TPU v7x, 32 devices: a whole 2x2x4 slice. The times are simulated.
32 devices in a mesh: groups: 2 (over y), src: 4 (over z), dst: 4 (over x, core).
Axes of the slice: x: 2, y: 2, z: 4, core: 2. Of those that a mesh axis runs over, the one named last changes fastest.
Arguments:
- source_table: float32 [16384, 400], P(('groups', 'src', 'dst')), parts along dimension 0
- source_state: float32 [16384], P(('groups', 'src', 'dst')), parts along dimension 0, may hold values from 0.01 to 0.5
- target_table: float32 [16384, 400], P(('groups', 'src', 'dst')), parts along dimension 0
- target_state: float32 [16384], P(('groups', 'src', 'dst')), parts along dimension 0, may hold values from 0.01 to 0.5
- relation_table: float32 [2560, 400], P('groups'), parts along dimension 0, may hold values from -6 to 6
- relation_state: float32 [2560], P('groups'), parts along dimension 0, may hold values from 0.01 to 0.5
- edge_list: int32 [3, 65536], P(None, ('groups', 'src', 'dst')), parts along dimension 1, may hold values from 0 to 1279, as said below
- edge_count: int32 [32], P(('groups', 'src', 'dst')), parts along dimension 0, may hold values from 1 to 2048, 10922 in all
- negative_ids: int32 [128, 512], P(('groups', 'src', 'dst')), parts along dimension 0, may hold values from 0 to 127
- source_lists: int32 [128, 64], P(('groups', 'src', 'dst')), parts along dimension 0, may hold values from 0 to 511
- target_lists: int32 [128, 32], P(('groups', 'src', 'dst')), parts along dimension 0, may hold values from 0 to 511
Outputs:
- new_source_table: float32 [16384, 400], P(('groups', 'src', 'dst')), parts along dimension 0
- new_source_state: float32 [16384], P(('groups', 'src', 'dst')), parts along dimension 0
- new_target_table: float32 [16384, 400], P(('groups', 'src', 'dst')), parts along dimension 0
- new_target_state: float32 [16384], P(('groups', 'src', 'dst')), parts along dimension 0
- new_relation_table: float32 [2560, 400], P('groups'), parts along dimension 0
- new_relation_state: float32 [2560], P('groups'), parts along dimension 0
There are 2 independent parts, one for each index of `groups`. A program takes and returns all parts, laid end to end along the dimension named above; each array names one. Nothing has to cross between parts.
Inputs may be any that keep to these rules, and one draw needn't show every extreme that they name: `edge_list`: row 0 is a slot among a bucket's 4 * 64 source slots, row 1 a relation, row 2 a slot among its 128 destination slots. Only the first edge_count edges of a bucket are live. `edge_count`: some bucket is full in every draw; every count is at least one. `negative_ids`: slots among a bucket's destination slots; repeats allowed. `source_lists`: local row numbers of the owner; repeats allowed. `target_lists`: local row numbers of the owner; repeats allowed.
All inputs are finite; a program needn't handle non-finite values. No bound on the sum of `edge_count` on one device may be relied on, other than what follows from the above.
Results may differ from a plain program's by a relative error of at most 0.0028.
Values may be sent and summed in bfloat16 or wider, within the bound.
A program may use at most 64 MiB of HBM per device.

v0:
```python
import jax
import jax.numpy as jnp
from jax import lax
from jax.sharding import PartitionSpec as P

learn_rate = 0.1


def complex_product(first_factor, second_factor):
    half_width = first_factor.shape[-1] // 2
    first_real = first_factor[..., :half_width]
    first_imag = first_factor[..., half_width:]
    second_real = second_factor[..., :half_width]
    second_imag = second_factor[..., half_width:]
    return jnp.concatenate(
        [
            first_real * second_real - first_imag * second_imag,
            first_real * second_imag + first_imag * second_real,
        ],
        axis=-1,
    )


def conjugate(values):
    half_width = values.shape[-1] // 2
    return jnp.concatenate([values[..., :half_width], -values[..., half_width:]], axis=-1)


def add_by_slot(accum, slots, grad):
    columns = jnp.arange(accum.shape[0], dtype=jnp.int32)
    indicator = (slots[:, None] == columns[None, :]).astype(jnp.bfloat16)
    grad_high = grad.astype(jnp.bfloat16)
    grad_rest = (grad - grad_high.astype(jnp.float32)).astype(jnp.bfloat16)
    dims = (((0,), (0,)), ((), ()))
    high_part = lax.dot_general(indicator, grad_high, dims, preferred_element_type=jnp.float32)
    rest_part = lax.dot_general(indicator, grad_rest, dims, preferred_element_type=jnp.float32)
    return accum + (high_part + rest_part)


def block_terms(source, relation, target, negatives, alive_mask):
    query_row = complex_product(source, relation)
    query_low = query_row.astype(jnp.bfloat16)
    positive = jnp.sum(query_row * target, axis=1)
    negative = lax.dot_general(
        query_low, negatives, (((1,), (1,)), ((), ())), preferred_element_type=jnp.float32
    )
    pos_weight = -alive_mask * jax.nn.sigmoid(-positive)
    neg_weight = (jax.nn.sigmoid(negative) * (alive_mask[:, None] / negatives.shape[0])).astype(
        jnp.bfloat16
    )
    query_grad = pos_weight[:, None] * target + jnp.dot(
        neg_weight, negatives, preferred_element_type=jnp.float32
    )
    target_grad = pos_weight[:, None] * query_row
    negative_grad = lax.dot_general(
        neg_weight, query_low, (((0,), (0,)), ((), ())), preferred_element_type=jnp.float32
    )
    source_grad = complex_product(query_grad, conjugate(relation))
    relation_grad = complex_product(query_grad, conjugate(source))
    return (source_grad, target_grad, negative_grad, relation_grad)


def row_update(table, state, grad):
    new_state = state + jnp.mean(grad * grad, axis=1)
    return (table - learn_rate * grad / jnp.sqrt(new_state)[:, None], new_state)


def body(
    source_table,
    source_state,
    target_table,
    target_state,
    relation_table,
    relation_state,
    edge_list,
    edge_count,
    negative_ids,
    source_lists,
    target_lists,
):
    row_width = source_table.shape[1]
    peers_row = lax.axis_size("dst")
    peers_column = lax.axis_size("src")
    cap_source = source_lists.shape[1]
    cap_target = target_lists.shape[1]
    source_out = (
        source_table[source_lists.reshape(-1)]
        .astype(jnp.bfloat16)
        .reshape(peers_row, cap_source, row_width)
    )
    src_rows = lax.all_to_all(source_out, "dst", split_axis=0, concat_axis=0, tiled=True).reshape(
        peers_row * cap_source, row_width
    )
    target_out = (
        target_table[target_lists.reshape(-1)]
        .astype(jnp.bfloat16)
        .reshape(peers_column, cap_target, row_width)
    )
    dst_rows = lax.all_to_all(target_out, "src", split_axis=0, concat_axis=0, tiled=True).reshape(
        peers_column * cap_target, row_width
    )
    live_count = edge_count[0]
    blocks = negative_ids.shape[0]
    block_rows = edge_list.shape[1] // blocks

    def one_block(block_index, carried):
        source_acc, target_acc, relation_acc = carried
        block_edges = lax.dynamic_slice_in_dim(edge_list, block_index * block_rows, block_rows, 1)
        position = block_index * block_rows + jnp.arange(block_rows, dtype=jnp.int32)
        alive_mask = (position < live_count).astype(jnp.float32)
        source = src_rows[block_edges[0]].astype(jnp.float32)
        relation = relation_table[block_edges[1]]
        target = dst_rows[block_edges[2]].astype(jnp.float32)
        negative_slots = lax.dynamic_index_in_dim(negative_ids, block_index, 0, keepdims=False)
        negatives = dst_rows[negative_slots]
        source_grad, target_grad, negative_grad, relation_grad = block_terms(
            source, relation, target, negatives, alive_mask
        )
        source_acc = add_by_slot(source_acc, block_edges[0], source_grad)
        target_acc = add_by_slot(target_acc, block_edges[2], target_grad)
        target_acc = add_by_slot(target_acc, negative_slots, negative_grad)
        relation_acc = add_by_slot(relation_acc, block_edges[1], relation_grad)
        return (source_acc, target_acc, relation_acc)

    initial = (
        jnp.zeros((peers_row * cap_source, row_width), jnp.float32),
        jnp.zeros((peers_column * cap_target, row_width), jnp.float32),
        jnp.zeros(relation_table.shape, jnp.float32),
    )
    source_slot_grad, target_slot_grad, relation_grad = lax.fori_loop(0, blocks, one_block, initial)
    source_back = lax.all_to_all(
        source_slot_grad.reshape(peers_row, cap_source, row_width),
        "dst",
        split_axis=0,
        concat_axis=0,
        tiled=True,
    )
    source_sum = (
        jnp.zeros_like(source_table)
        .at[source_lists.reshape(-1)]
        .add(source_back.reshape(-1, row_width))
    )
    target_back = lax.all_to_all(
        target_slot_grad.reshape(peers_column, cap_target, row_width),
        "src",
        split_axis=0,
        concat_axis=0,
        tiled=True,
    )
    target_sum = (
        jnp.zeros_like(target_table)
        .at[target_lists.reshape(-1)]
        .add(target_back.reshape(-1, row_width))
    )
    new_source_table, new_source_state = row_update(source_table, source_state, source_sum)
    new_target_table, new_target_state = row_update(target_table, target_state, target_sum)
    relation_total = lax.psum(relation_grad, ("src", "dst"))
    new_relation_table, new_relation_state = row_update(
        relation_table, relation_state, relation_total
    )
    return (
        new_source_table,
        new_source_state,
        new_target_table,
        new_target_state,
        new_relation_table,
        new_relation_state,
    )


def solution(mesh):
    placed = (
        P(("groups", "src", "dst"), None),
        P(("groups", "src", "dst")),
        P(("groups", "src", "dst"), None),
        P(("groups", "src", "dst")),
        P("groups", None),
        P("groups"),
        P(None, ("groups", "src", "dst")),
        P(("groups", "src", "dst")),
        P(("groups", "src", "dst"), None),
        P(("groups", "src", "dst"), None),
        P(("groups", "src", "dst"), None),
    )
    return jax.shard_map(
        body,
        mesh=mesh,
        in_specs=placed,
        out_specs=(
            P(("groups", "src", "dst"), None),
            P(("groups", "src", "dst")),
            P(("groups", "src", "dst"), None),
            P(("groups", "src", "dst")),
            P("groups", None),
            P("groups"),
        ),
        check_vma=False,
    )
```

profile of v0, /device:TPU:0, one launch (start us, length us, event | category | flops | bytes accessed | tf_op | source)
XLA Modules:
  0.0 309.3 jit_solution(8680711712426035579)
XLA Ops:
  11.2 4.2 %all-to-all-start = ((bf16[4,64,400]{2,1,0:T(8,128)(2,1)}), bf16[4,64,400]{2,1,0:T(8,128)(2,1)S(1)}, u32[]{:S(2)}, u32[]{:S(2)}) async-start(bf16[4,64,400]{2,1,0:T(8,128)(2,1)} %bitcast.2), calls=%async_computation | async-start | bytes 524288 | tf_op jit(solution)/shard_map/all_to_all | solution.py:91
  17.3 4.2 %all-to-all-done = bf16[4,64,400]{2,1,0:T(8,128)(2,1)S(1)} async-done(((bf16[4,64,400]{2,1,0:T(8,128)(2,1)}), bf16[4,64,400]{2,1,0:T(8,128)(2,1)S(1)}, u32[]{:S(2)}, u32[]{:S(2)}) %all-to-all-start) | async-done | bytes 204832 | tf_op jit(solution)/shard_map/all_to_all | solution.py:91
  21.5 5.5 %all-to-all-start.1 = ((bf16[4,32,400]{2,1,0:T(8,128)(2,1)}), bf16[4,32,400]{2,1,0:T(8,128)(2,1)S(1)}, u32[]{:S(2)}, u32[]{:S(2)}) async-start(bf16[4,32,400]{2,1,0:T(8,128)(2,1)} %bitcast.5), calls=%async_computation.1 | async-start | bytes 262144 | tf_op jit(solution)/shard_map/all_to_all | solution.py:99
  29.0 4.0 %all-to-all-done.1 = bf16[4,32,400]{2,1,0:T(8,128)(2,1)S(1)} async-done(((bf16[4,32,400]{2,1,0:T(8,128)(2,1)}), bf16[4,32,400]{2,1,0:T(8,128)(2,1)S(1)}, u32[]{:S(2)}, u32[]{:S(2)}) %all-to-all-start.1) | async-done | bytes 102432 | tf_op jit(solution)/shard_map/all_to_all | solution.py:99
  33.0 142.9 %while.18 = (s32[]{:T(128)}, f32[256,400]{0,1:T(8,128)}, f32[128,400]{0,1:T(8,128)}, f32[1280,400]{0,1:T(8,128)}, s32[3,2048]{1,0:T(4,128)}, /*index=5*/s32[]{:T...) while((s32[]{:T(128)}, f32[256,400]{0,1:T(8,128)}, ...), condition=%wide.region_2.3_spmd.clone, body=%wide.region_0.2_spmd.clone.sunk | while | flops 2114290176 | bytes 70885896 | solution.py:130
  34.6 2.6 gather_fusion
  37.3 2.6 gather_fusion.3
  41.1 2.6 gather_fusion.2
  70.3 2.6 gather_fusion
  73.0 2.6 gather_fusion.3
  76.8 2.6 gather_fusion.2
  106.1 2.6 gather_fusion
  108.7 2.6 gather_fusion.3
  112.5 2.6 gather_fusion.2
  141.8 2.6 gather_fusion
  144.4 2.6 gather_fusion.3
  148.2 2.6 gather_fusion.2
  177.9 3.7 %all-to-all-start.2 = ((f32[4,64,400]{2,1,0:T(8,128)}), f32[4,64,400]{2,1,0:T(8,128)S(1)}, u32[]{:S(2)}, u32[]{:S(2)}) async-start(f32[4,64,400]{2,1,0:T(8,128)} %bitcast.7), calls=%async_computation.2 | async-start | bytes 1048576 | tf_op jit(solution)/shard_map/all_to_all | solution.py:131
  182.4 8.0 %all-to-all-done.2 = f32[4,64,400]{2,1,0:T(8,128)S(1)} async-done(((f32[4,64,400]{2,1,0:T(8,128)}), f32[4,64,400]{2,1,0:T(8,128)S(1)}, u32[]{:S(2)}, u32[]{:S(2)}) %all-to-all-start.2) | async-done | bytes 409632 | tf_op jit(solution)/shard_map/all_to_all | solution.py:131
  190.4 3.4 %all-to-all-start.3 = ((f32[4,32,400]{2,1,0:T(8,128)}), f32[4,32,400]{2,1,0:T(8,128)S(1)}, u32[]{:S(2)}, u32[]{:S(2)}) async-start(f32[4,32,400]{2,1,0:T(8,128)} %bitcast.9), calls=%async_computation.3 | async-start | bytes 524288 | tf_op jit(solution)/shard_map/all_to_all | solution.py:143
  197.1 5.7 %all-to-all-done.3 = f32[4,32,400]{2,1,0:T(8,128)S(1)} async-done(((f32[4,32,400]{2,1,0:T(8,128)}), f32[4,32,400]{2,1,0:T(8,128)S(1)}, u32[]{:S(2)}, u32[]{:S(2)}) %all-to-all-start.3) | async-done | bytes 204832 | tf_op jit(solution)/shard_map/all_to_all | solution.py:143
  206.6 2.5 copy.35
  210.5 86.5 %all-reduce.2.cloned.1.call-done = f32[1280,400]{0,1:T(8,128)} async-done(((f32[1280,400]{0,1:T(8,128)}), f32[1280,400]{0,1:T(8,128)}) %all-reduce.2.cloned.1.call-update) | async-done | bytes 2048016 | tf_op jit(solution)/shard_map/psum | solution.py:157
  299.3 3.1 %divide_subtract_fusion = f32[1280,400]{0,1:T(8,128)} fusion(f32[1280,400]{0,1:T(8,128)S(1)} %copy-done.14, f32[1280,400]{0,1:T(8,128)} %all-reduce.2.cloned.1.call-done, f32[1280]{0:T(1024)S(1)} %get-tuple-element.267), kind=kLoop, calls=%fused_computation.85 | loop fusion | flops 1536000 | bytes 6149120 | tf_op jit(solution)/shard_map/sub | solution.py:65
  (238 shorter events, 131.9 us)
Async XLA Ops:
  7.9 7.5 %copy-start.19 = (s32[4,32]{1,0:T(4,128)S(1)}, s32[4,32]{1,0:T(4,128)}, u32[]{:S(2)}) copy-start(s32[4,32]{1,0:T(4,128)} %param.23) | copy-start | bytes 1540
  8.0 7.6 %copy-start.17 = (f32[512,400]{0,1:T(8,128)S(1)}, f32[512,400]{0,1:T(8,128)}, u32[]{:S(2)}) copy-start(f32[512,400]{0,1:T(8,128)} %param.15) | copy-start | bytes 2457604
  11.2 10.2 %all-to-all-start = ((bf16[4,64,400]{2,1,0:T(8,128)(2,1)}), bf16[4,64,400]{2,1,0:T(8,128)(2,1)S(1)}, u32[]{:S(2)}, u32[]{:S(2)}) async-start(bf16[4,64,400]{2,1,0:T(8,128)(2,1)} %bitcast.2), calls=%async_computation | async-start | bytes 524288 | tf_op jit(solution)/shard_map/all_to_all | solution.py:91
  15.9 5.6 %copy-start.10 = (f32[512,400]{1,0:T(8,128)}, f32[512,400]{1,0:T(8,128)S(1)}, u32[]{:S(2)}) copy-start(f32[512,400]{1,0:T(8,128)S(1)} %copy.29) | copy-start | bytes 2457604
  21.5 11.6 %all-to-all-start.1 = ((bf16[4,32,400]{2,1,0:T(8,128)(2,1)}), bf16[4,32,400]{2,1,0:T(8,128)(2,1)S(1)}, u32[]{:S(2)}, u32[]{:S(2)}) async-start(bf16[4,32,400]{2,1,0:T(8,128)(2,1)} %bitcast.5), calls=%async_computation.1 | async-start | bytes 262144 | tf_op jit(solution)/shard_map/all_to_all | solution.py:99
  56.4 2.8 copy-start.15
  64.8 2.6 copy-start.9
  92.1 2.8 copy-start.15
  100.5 2.6 copy-start.9
  127.9 2.8 copy-start.15
  136.2 2.6 copy-start.9
  163.6 2.8 copy-start.15
  171.9 2.6 copy-start.9
  175.9 5.7 %copy-start.16 = (f32[128,400]{0,1:T(8,128)S(1)}, f32[128,400]{0,1:T(8,128)}, u32[]{:S(2)}) copy-start(f32[128,400]{0,1:T(8,128)} %get-tuple-element.178) | copy-start | bytes 614404
  177.9 12.5 %all-to-all-start.2 = ((f32[4,64,400]{2,1,0:T(8,128)}), f32[4,64,400]{2,1,0:T(8,128)S(1)}, u32[]{:S(2)}, u32[]{:S(2)}) async-start(f32[4,64,400]{2,1,0:T(8,128)} %bitcast.7), calls=%async_computation.2 | async-start | bytes 1048576 | tf_op jit(solution)/shard_map/all_to_all | solution.py:131
  190.4 12.4 %all-to-all-start.3 = ((f32[4,32,400]{2,1,0:T(8,128)}), f32[4,32,400]{2,1,0:T(8,128)S(1)}, u32[]{:S(2)}, u32[]{:S(2)}) async-start(f32[4,32,400]{2,1,0:T(8,128)} %bitcast.9), calls=%async_computation.3 | async-start | bytes 524288 | tf_op jit(solution)/shard_map/all_to_all | solution.py:143
  193.8 103.2 %all-reduce.2.cloned.1.call-start = ((), (), s32[]{:S(2)}) async-start(), calls=%async_computation.4 | async-start | bytes 4096000 | tf_op jit(solution)/shard_map/psum | solution.py:157
  194.5 10.0 %copy-start.20 = (f32[512]{0:T(512)S(1)}, f32[512]{0:T(512)}, u32[]{:S(2)}) copy-start(f32[512]{0:T(512)} %param.16) | copy-start | bytes 6148
  194.5 10.0 %copy-start.21 = (f32[512]{0:T(512)S(1)}, f32[512]{0:T(512)}, u32[]{:S(2)}) copy-start(f32[512]{0:T(512)} %param.14) | copy-start | bytes 6148
  194.6 10.8 %copy-start.7 = (f32[512,400]{1,0:T(8,128)S(1)}, f32[512,400]{1,0:T(8,128)}, u32[]{:S(2)}) copy-start(f32[512,400]{1,0:T(8,128)} %copy-done.6) | copy-start | bytes 2457604
  205.3 3.7 %copy-start.11 = (f32[512,400]{1,0:T(8,128)S(1)}, f32[512,400]{1,0:T(8,128)}, u32[]{:S(2)}) copy-start(f32[512,400]{1,0:T(8,128)} %copy-done.10) | copy-start | bytes 2457604
  206.5 2.5 copy-start.13
  209.3 89.5 %copy-start.18 = (f32[1280]{0:T(1024)S(1)}, f32[1280]{0:T(1024)}, u32[]{:S(2)}) copy-start(f32[1280]{0:T(1024)} %param.18) | copy-start | bytes 15364
  209.3 90.0 %copy-start.14 = (f32[1280,400]{0,1:T(8,128)S(1)}, f32[1280,400]{0,1:T(8,128)}, u32[]{:S(2)}) copy-start(f32[1280,400]{0,1:T(8,128)} %param.17) | copy-start | bytes 6144004
  (30 other events, 43.7 us)
Sparse Core Ops, SparseCore 0:
  198.8 98.1 all-reduce.1
where the time goes:
time: 312 us; the launch traced here: 309 us
  waiting for transfers between devices  109 us (35%)
  local copies, waits for them, and re-layouts  104 us (33%)
  other arithmetic  37.1 us (12%)
  matrix products  27.2 us (9%)
  starting transfers between devices  16.8 us (5%)
  between operations  14.2 us (5%)
    psum x1, waiting for transfers between devices, body(): relation_total = lax.psum(relation_grad, ('src', 'dst'))  86.5 us
    while x80, local copies, waits for them, and re-layouts  26.1 us
    gather x8, local copies, waits for them, and re-layouts, one_block(): source = src_rows[block_edges[0]].astype(jnp.float32)  18.5 us
    gather x8, local copies, waits for them, and re-layouts, one_block(): target = dst_rows[block_edges[2]].astype(jnp.float32)  15.4 us
    dot_general x16, matrix products, add_by_slot(): lax.dot_general(indicator, grad_rest, dims, preferred_element_type=jnp.fl...  13.5 us
    gather x4, local copies, waits for them, and re-layouts, one_block(): negatives = dst_rows[negative_slots]  10.5 us
    slice x4, local copies, waits for them, and re-layouts, complex_product(): second_imag = second_factor[..., half_width:]  9.67 us
    gather x4, local copies, waits for them, and re-layouts, one_block(): relation = relation_table[block_edges[1]]  9.32 us
  transfers between devices with their start and end apart: 5, of which 5 were waited for; matrix products, arithmetic and copies ran while one was open for 5% of the time, Pallas kernels for 0%

commit v1 on v0

v1 whole, which is shorter than its diff:
```python
import functools

import jax
import jax.numpy as jnp
from jax import lax
from jax.experimental import pallas as pl
from jax.experimental.pallas import tpu as pltpu
from jax.sharding import PartitionSpec as P

learn_rate = 0.1
MESH = pl.DeviceIdType.MESH
BF = jnp.bfloat16
F32 = jnp.float32


def dot(a, b):
    return jnp.dot(a, b, preferred_element_type=F32)


def dot_nt(a, b):
    return lax.dot_general(a, b, (((1,), (1,)), ((), ())), preferred_element_type=F32)


def dot_tn(a, b):
    return lax.dot_general(a, b, (((0,), (0,)), ((), ())), preferred_element_type=F32)


def one_hot(rows, ids):
    where = lax.broadcasted_iota(jnp.int32, (rows, ids.shape[1]), 0) == ids
    return jnp.where(where, 1.0, 0.0).astype(BF)


def greet(n_src, n_dst, me_s, me_d):
    barrier = pltpu.get_barrier_semaphore()
    for k in range(1, n_dst):
        pl.semaphore_signal(
            barrier, 1, device_id={"dst": lax.rem(me_d + k, n_dst)}, device_id_type=MESH
        )
    for k in range(1, n_src):
        pl.semaphore_signal(
            barrier, 1, device_id={"src": lax.rem(me_s + k, n_src)}, device_id_type=MESH
        )
    pl.semaphore_wait(barrier, n_src + n_dst - 2)


def swap(axis, n, me, cap, out_ref, in_ref, send, recv):
    copies = []
    for k in range(1, n):
        peer = lax.rem(me + k, n)
        copy = pltpu.make_async_remote_copy(
            src_ref=out_ref.at[pl.ds(pl.multiple_of(peer * cap, cap), cap)],
            dst_ref=in_ref.at[pl.ds(pl.multiple_of(me * cap, cap), cap)],
            send_sem=send.at[k - 1],
            recv_sem=recv.at[k - 1],
            device_id={axis: peer},
            device_id_type=MESH,
        )
        copy.start()
        copies.append(copy)
    return copies


def fetch_kernel(
    n_src, n_dst, stab, ttab, slist, tlist, srows, drows, sout, tout, sin, tin, s1, r1, s2, r2
):
    me_s = lax.axis_index("src")
    me_d = lax.axis_index("dst")
    cs = slist.shape[1]
    cd = tlist.shape[1]
    greet(n_src, n_dst, me_s, me_d)
    table = stab[...].astype(BF)
    for p in range(n_dst):
        sout[p * cs : (p + 1) * cs, :] = dot_tn(
            one_hot(table.shape[0], slist[p : p + 1, :]), table
        ).astype(BF)
    first = swap("dst", n_dst, me_d, cs, sout, sin, s1, r1)
    table = ttab[...].astype(BF)
    for p in range(n_src):
        tout[p * cd : (p + 1) * cd, :] = dot_tn(
            one_hot(table.shape[0], tlist[p : p + 1, :]), table
        ).astype(BF)
    second = swap("src", n_src, me_s, cd, tout, tin, s2, r2)
    mine = pl.ds(pl.multiple_of(me_d * cs, cs), cs)
    sin[mine, :] = sout[mine, :]
    mine = pl.ds(pl.multiple_of(me_s * cd, cd), cd)
    tin[mine, :] = tout[mine, :]
    for copy in first:
        copy.wait()
    srows[...] = sin[...]
    for copy in second:
        copy.wait()
    drows[...] = tin[...]


def bucket_kernel(
    srows, drows, rel, edges, count, negs, sgrad, tgrad, rgrad, rel_hi, rel_lo, src_t, dst_t, hots, rg
):
    slots = srows.shape[0]
    targets = drows.shape[0]
    relations, width = rel.shape
    half = width // 2
    blocks, negatives = negs.shape
    span = edges.shape[1] // blocks
    table = rel[...]
    high = table.astype(BF)
    rel_hi[...] = high.T
    rel_lo[...] = (table - high.astype(F32)).astype(BF).T
    src_t[...] = srows[...].T
    dst_t[...] = drows[...].T
    source_acc = jnp.zeros((slots, width), F32)
    target_acc = jnp.zeros((targets, width), F32)
    live = count[0]
    for c in range(blocks):
        cols = slice(c * span, (c + 1) * span)
        uses = one_hot(targets, negs[c : c + 1, :])
        uses = jnp.sum(uses.astype(F32), axis=1, keepdims=True)
        hot_s = one_hot(slots, edges[0:1, cols])
        hot_r = one_hot(relations, edges[1:2, cols])
        hots[:, cols] = hot_r
        is_target = (
            lax.broadcasted_iota(jnp.int32, (targets, span), 0) == edges[2:3, cols]
        )
        place = c * span + lax.broadcasted_iota(jnp.int32, (1, span), 1)
        alive = jnp.where(place < live, 1.0, 0.0)
        source = dot(src_t[...], hot_s)
        relation = dot(rel_hi[...], hot_r) + dot(rel_lo[...], hot_r)
        sr, si = source[:half], source[half:]
        rr, ri = relation[:half], relation[half:]
        query = jnp.concatenate([sr * rr - si * ri, sr * ri + si * rr], axis=0)
        low = query.astype(BF)
        rest = (query - low.astype(F32)).astype(BF)
        logits = dot(drows[...], low)
        extra = dot(drows[...], rest)
        positive = jnp.sum(jnp.where(is_target, logits + extra, 0.0), axis=0, keepdims=True)
        pos_weight = -alive * jax.nn.sigmoid(-positive)
        neg_weight = (jax.nn.sigmoid(logits) * (alive / negatives)).astype(BF).astype(F32)
        weight = jnp.where(is_target, pos_weight, 0.0) + uses * neg_weight
        w_high = weight.astype(BF)
        w_rest = (weight - w_high.astype(F32)).astype(BF)
        grad = dot(dst_t[...], w_high) + dot(dst_t[...], w_rest)
        target_acc = target_acc + (
            dot_nt(w_high, low) + (dot_nt(w_rest, low) + dot_nt(w_high, rest))
        )
        gr, gi = grad[:half], grad[half:]
        source_grad = jnp.concatenate([gr * rr + gi * ri, gi * rr - gr * ri], axis=0)
        source_acc = source_acc + dot_nt(hot_s, source_grad.astype(BF))
        rg[:, cols] = jnp.concatenate(
            [gr * sr + gi * si, gi * sr - gr * si], axis=0
        ).astype(BF)
    sgrad[...] = source_acc.astype(BF)
    tgrad[...] = target_acc.astype(BF)
    rgrad[0:relations, :] = dot_nt(hots[...], rg[...]).astype(BF)
    if rgrad.shape[0] > relations:
        rgrad[relations:, :] = jnp.zeros((rgrad.shape[0] - relations, width), BF)


def return_kernel(
    n_src, n_dst, pieces, step,
    sgrad, tgrad, rgrad, slist, tlist,
    ssum, tsum, total,
    sin, tin, core_in, x_in, z_in, core_sum, x_sum, full,
    s1, r1, s2, r2, cs_s, cs_r, xs_s, xs_r, zs_s, zs_r, zg_s, zg_r, xg_s, xg_r, cg_s, cg_r,
):
    me_s = lax.axis_index("src")
    me_d = lax.axis_index("dst")
    core = lax.rem(me_d, 2)
    chip = me_d // 2
    chips = n_dst // 2
    cs = slist.shape[1]
    cd = tlist.shape[1]
    z_rows = step
    x_rows = z_rows * n_src
    c_rows = x_rows * chips
    p_rows = c_rows * 2

    def rows(start, count):
        return pl.ds(pl.multiple_of(start, 16), count)

    def push(src, dst, send, recv, axis, peer):
        copy = pltpu.make_async_remote_copy(
            src_ref=src, dst_ref=dst, send_sem=send, recv_sem=recv,
            device_id={axis: peer}, device_id_type=MESH,
        )
        copy.start()
        return copy

    greet(n_src, n_dst, me_s, me_d)
    other = me_d + 1 - 2 * core
    started = {}
    for p in range(pieces):
        started["c", p] = [
            push(
                rgrad.at[rows(p * p_rows + (1 - core) * c_rows, c_rows)],
                core_in.at[pl.ds(p * c_rows, c_rows)],
                cs_s.at[p], cs_r.at[p], "dst", other,
            )
        ]
    first = swap("dst", n_dst, me_d, cs, sgrad, sin, s1, r1)
    second = swap("src", n_src, me_s, cd, tgrad, tin, s2, r2)
    mine = pl.ds(pl.multiple_of(me_d * cs, cs), cs)
    sin[mine, :] = sgrad[mine, :]
    mine = pl.ds(pl.multiple_of(me_s * cd, cd), cd)
    tin[mine, :] = tgrad[mine, :]

    def stage_x(p):
        for copy in started["c", p]:
            copy.wait()
        here = pl.ds(p * c_rows, c_rows)
        own = rgrad[rows(p * p_rows + core * c_rows, c_rows), :]
        core_sum[here, :] = (own.astype(F32) + core_in[here, :].astype(F32)).astype(BF)
        started["x", p] = []
        for k in range(1, chips):
            peer = lax.rem(chip + k, chips)
            slot = p * (chips - 1) + k - 1
            started["x", p].append(
                push(
                    core_sum.at[rows(p * c_rows + peer * x_rows, x_rows)],
                    x_in.at[pl.ds(slot * x_rows, x_rows)],
                    xs_s.at[slot], xs_r.at[slot], "dst", peer * 2 + core,
                )
            )

    def stage_z(p):
        for copy in started["x", p]:
            copy.wait()
        value = core_sum[rows(p * c_rows + chip * x_rows, x_rows), :].astype(F32)
        for k in range(1, chips):
            slot = p * (chips - 1) + k - 1
            value = value + x_in[pl.ds(slot * x_rows, x_rows), :].astype(F32)
        x_sum[pl.ds(p * x_rows, x_rows), :] = value.astype(BF)
        started["z", p] = []
        for k in range(1, n_src):
            peer = lax.rem(me_s + k, n_src)
            slot = p * (n_src - 1) + k - 1
            started["z", p].append(
                push(
                    x_sum.at[rows(p * x_rows + peer * z_rows, z_rows)],
                    z_in.at[pl.ds(slot * z_rows, z_rows)],
                    zs_s.at[slot], zs_r.at[slot], "src", peer,
                )
            )

    def place(p, chip_at, src_at):
        return p * p_rows + core * c_rows + chip_at * x_rows + src_at * z_rows

    def gather_z(p):
        for copy in started["z", p]:
            copy.wait()
        value = x_sum[rows(p * x_rows + me_s * z_rows, z_rows), :].astype(F32)
        for k in range(1, n_src):
            slot = p * (n_src - 1) + k - 1
            value = value + z_in[pl.ds(slot * z_rows, z_rows), :].astype(F32)
        here = rows(place(p, chip, me_s), z_rows)
        full[here, :] = value.astype(BF)
        started["gz", p] = []
        for k in range(1, n_src):
            peer = lax.rem(me_s + k, n_src)
            slot = p * (n_src - 1) + k - 1
            started["gz", p].append(
                push(full.at[here], full.at[here], zg_s.at[slot], zg_r.at[slot], "src", peer)
            )

    def gather_x(p):
        for copy in started["gz", p]:
            copy.wait()
        here = rows(place(p, chip, 0), x_rows)
        started["gx", p] = []
        for k in range(1, chips):
            peer = lax.rem(chip + k, chips)
            slot = p * (chips - 1) + k - 1
            started["gx", p].append(
                push(
                    full.at[here], full.at[here], xg_s.at[slot], xg_r.at[slot],
                    "dst", peer * 2 + core,
                )
            )

    def gather_core(p):
        for copy in started["gx", p]:
            copy.wait()
        here = rows(place(p, 0, 0), c_rows)
        started["gc", p] = [
            push(full.at[here], full.at[here], cg_s.at[p], cg_r.at[p], "dst", other)
        ]

    def sums():
        for copy in first:
            copy.wait()
        value = jnp.zeros(ssum.shape, F32)
        for p in range(n_dst):
            value = value + dot(
                one_hot(ssum.shape[0], slist[p : p + 1, :]), sin[p * cs : (p + 1) * cs, :]
            )
        ssum[...] = value
        for copy in second:
            copy.wait()
        value = jnp.zeros(tsum.shape, F32)
        for p in range(n_src):
            value = value + dot(
                one_hot(tsum.shape[0], tlist[p : p + 1, :]), tin[p * cd : (p + 1) * cd, :]
            )
        tsum[...] = value

    stages = [stage_x, stage_z, gather_z, gather_x, gather_core]
    for t in range(pieces + len(stages) - 1):
        for s in reversed(range(len(stages))):
            if 0 <= t - s < pieces:
                stages[s](t - s)
        if t == pieces - 1:
            sums()
    for p in range(pieces):
        for copy in started["gc", p]:
            copy.wait()
    total[...] = full[0 : total.shape[0], :]


def update_rows(table, state, grad):
    new_state = state + jnp.mean(grad * grad, axis=1)
    return (table - learn_rate * grad / jnp.sqrt(new_state)[:, None], new_state)


VM = pl.BlockSpec(memory_space=pltpu.VMEM)
SM = pl.BlockSpec(memory_space=pltpu.SMEM)
LIMIT = 48 * 1024 * 1024


def body(
    source_table, source_state, target_table, target_state, relation_table, relation_state,
    edge_list, edge_count, negative_ids, source_lists, target_lists,
):
    n_dst = lax.axis_size("dst")
    n_src = lax.axis_size("src")
    width = source_table.shape[1]
    cs = source_lists.shape[1]
    cd = target_lists.shape[1]
    own = source_table.shape[0]
    relations = relation_table.shape[0]
    group = n_src * n_dst
    share = -(-relations // (group * 16)) * 16
    step = 16
    pieces = share // step
    padded = share * group
    slots, targets = n_dst * cs, n_src * cd
    dma = pltpu.SemaphoreType.DMA

    src_rows, dst_rows = pl.pallas_call(
        functools.partial(fetch_kernel, n_src, n_dst),
        out_shape=[
            jax.ShapeDtypeStruct((slots, width), BF),
            jax.ShapeDtypeStruct((targets, width), BF),
        ],
        in_specs=[VM] * 4,
        out_specs=[VM] * 2,
        scratch_shapes=[
            pltpu.VMEM((slots, width), BF),
            pltpu.VMEM((targets, width), BF),
            pltpu.VMEM((slots, width), BF),
            pltpu.VMEM((targets, width), BF),
            dma((n_dst - 1,)), dma((n_dst - 1,)), dma((n_src - 1,)), dma((n_src - 1,)),
        ],
        compiler_params=pltpu.CompilerParams(
            collective_id=0, has_side_effects=True, vmem_limit_bytes=LIMIT
        ),
        name="fetch",
    )(source_table, target_table, source_lists, target_lists)

    edges = edge_list.shape[1]
    sgrad, tgrad, rgrad = pl.pallas_call(
        bucket_kernel,
        out_shape=[
            jax.ShapeDtypeStruct((slots, width), BF),
            jax.ShapeDtypeStruct((targets, width), BF),
            jax.ShapeDtypeStruct((padded, width), BF),
        ],
        in_specs=[VM, VM, VM, VM, SM, VM],
        out_specs=[VM] * 3,
        scratch_shapes=[
            pltpu.VMEM((width, relations), BF),
            pltpu.VMEM((width, relations), BF),
            pltpu.VMEM((width, slots), BF),
            pltpu.VMEM((width, targets), BF),
            pltpu.VMEM((relations, edges), BF),
            pltpu.VMEM((width, edges), BF),
        ],
        compiler_params=pltpu.CompilerParams(vmem_limit_bytes=LIMIT),
        name="bucket",
    )(src_rows, dst_rows, relation_table, edge_list, edge_count, negative_ids)

    chips = n_dst // 2
    x_rows = step * n_src
    c_rows = x_rows * chips
    core_n = pieces
    x_n = pieces * (chips - 1)
    z_n = pieces * (n_src - 1)
    source_sum, target_sum, relation_total = pl.pallas_call(
        functools.partial(return_kernel, n_src, n_dst, pieces, step),
        out_shape=[
            jax.ShapeDtypeStruct((own, width), F32),
            jax.ShapeDtypeStruct((target_table.shape[0], width), F32),
            jax.ShapeDtypeStruct((relations, width), BF),
        ],
        in_specs=[VM] * 5,
        out_specs=[VM] * 3,
        scratch_shapes=[
            pltpu.VMEM((slots, width), BF),
            pltpu.VMEM((targets, width), BF),
            pltpu.VMEM((pieces * c_rows, width), BF),
            pltpu.VMEM((x_n * x_rows, width), BF),
            pltpu.VMEM((z_n * step, width), BF),
            pltpu.VMEM((pieces * c_rows, width), BF),
            pltpu.VMEM((pieces * x_rows, width), BF),
            pltpu.VMEM((padded, width), BF),
            dma((n_dst - 1,)), dma((n_dst - 1,)), dma((n_src - 1,)), dma((n_src - 1,)),
            dma((core_n,)), dma((core_n,)), dma((x_n,)), dma((x_n,)), dma((z_n,)), dma((z_n,)),
            dma((z_n,)), dma((z_n,)), dma((x_n,)), dma((x_n,)), dma((core_n,)), dma((core_n,)),
        ],
        compiler_params=pltpu.CompilerParams(
            collective_id=1, has_side_effects=True, vmem_limit_bytes=LIMIT
        ),
        name="give_back",
    )(sgrad, tgrad, rgrad, source_lists, target_lists)

    new_source_table, new_source_state = update_rows(source_table, source_state, source_sum)
    new_target_table, new_target_state = update_rows(target_table, target_state, target_sum)
    new_relation_table, new_relation_state = update_rows(
        relation_table, relation_state, relation_total.astype(F32)
    )
    return (
        new_source_table, new_source_state, new_target_table, new_target_state,
        new_relation_table, new_relation_state,
    )


def solution(mesh):
    every = ("groups", "src", "dst")
    rows = P(every, None)
    flat = P(every)
    outs = (rows, flat, rows, flat, P("groups", None), P("groups"))
    return jax.shard_map(
        body,
        mesh=mesh,
        in_specs=outs + (P(None, every), flat, rows, rows, rows),
        out_specs=outs,
        check_vma=False,
    )
```

time: 312 us -> 85.6 us (0.27)
  waiting for transfers between devices: 109 us -> 0 us
  local copies, waits for them, and re-layouts: 104 us -> 12.2 us
  Pallas kernels: 0 us -> 62.7 us
  other arithmetic: 37.1 us -> 8.81 us
  matrix products: 27.2 us -> 0 us
  starting transfers between devices: 16.8 us -> 0 us
  between operations: 14.2 us -> 1.5 us
    psum x1 -> x0, waiting for transfers between devices: 86.5 us -> none  [body(): relation_total = lax.psum(relation_grad, ('src', 'dst'))]
    pallas_call x0 -> x3, Pallas kernels: none -> 62.7 us  [the longest x1 40.1 us: body(): pl.pallas_call(functools.partial(return_kernel, n_src, n_dst, pieces, ste...]
    gather x26 -> x0, local copies, waits for them, and re-layouts: 56.7 us -> none  [the longest x8 18.5 us: one_block(): source = src_rows[block_edges[0]].astype(jnp.float32)]
    while x82 -> x0, local copies, waits for them, and re-layouts: 29 us -> none
    dot_general x44 -> x0, matrix products: 27.2 us -> none  [the longest x16 13.5 us: add_by_slot(): lax.dot_general(indicator, grad_rest, dims, preferred_element_type=jnp.fl...]
    all_to_all x4 -> x0, waiting for transfers between devices: 21.8 us -> none  [the longest x1 7.96 us: body(): lax.all_to_all(source_slot_grad.reshape(peers_row, cap_source, row_width)...]
    all_to_all x4 -> x0, starting transfers between devices: 16.8 us -> none  [the longest x1 5.49 us: body(): lax.all_to_all(target_out, 'src', split_axis=0, concat_axis=0, tiled=True)]
    slice x4 -> x0, local copies, waits for them, and re-layouts: 9.67 us -> none  [complex_product(): second_imag = second_factor[..., half_width:]]
  transfers between devices with their start and end apart: 5 -> 0, of which waited for: 5 -> 0; matrix products, arithmetic and copies ran while one was open for 5% -> 0% of each run, Pallas kernels for 0% -> 0%
where the time goes in v1:
time: 85.6 us; the launch traced here: 85.3 us
  Pallas kernels  62.7 us (73%)
  local copies, waits for them, and re-layouts  12.2 us (14%)
  other arithmetic  8.81 us (10%)
  between operations  1.5 us (2%)
    pallas_call x1, Pallas kernels, body(): pl.pallas_call(functools.partial(return_kernel, n_src, n_dst, pieces, ste...  40.1 us
    pallas_call x1, Pallas kernels, body(): pl.pallas_call(bucket_kernel, out_shape=[jax.ShapeDtypeStruct((slots, wid...  12.7 us
    unnamed x32, local copies, waits for them, and re-layouts  12.2 us
    pallas_call x1, Pallas kernels, body(): pl.pallas_call(functools.partial(fetch_kernel, n_src, n_dst), out_shape=[...  9.91 us
    sub x2, other arithmetic, update_rows(): return (table - learn_rate * grad / jnp.sqrt(new_state)[:, None], new_state)  4.98 us
    reduce_sum x3, other arithmetic, update_rows(): new_state = state + jnp.mean(grad * grad, axis=1)  1.97 us
    sqrt x3, other arithmetic, update_rows(): return (table - learn_rate * grad / jnp.sqrt(new_state)[:, None], new_state)  1.87 us

profile of v1, /device:TPU:0, one launch (start us, length us, event | category | flops | bytes accessed | tf_op | source)
XLA Modules:
  0.0 85.3 jit_solution(6084274432685225525)
XLA Ops:
  1.3 1.5 %copy.20.stab = f32[512,400]{1,0:T(8,128)S(1)} copy(f32[512,400]{0,1:T(8,128)} %param.11) | data formatting | bytes 1638400 | tf_op args[0]
  2.8 1.9 %copy.18.ttab = f32[512,400]{1,0:T(8,128)S(1)} copy(f32[512,400]{0,1:T(8,128)} %param.13) | data formatting | bytes 1638400 | tf_op args[2]
  4.7 9.9 %fetch.1 = (bf16[256,400]{1,0:T(8,128)(2,1)S(1)}, bf16[128,400]{1,0:T(8,128)(2,1)S(1)}) custom-call(f32[512,400]{1,0:T(8,128)S(1)} %copy.20.stab, f32[512,400]{1,0:T(8,128)S(1)} %copy.18.ttab, s32[4,64]{1,0:T(4,128)S(1)} %copy-done.7, s32[4,32]{1,0:T(4,128)S(1)} %copy-done.8), custom_call_target="tpu_custom_call" | custom-call | tf_op jit(solution)/shard_map/fetch/pallas_call | solution.py:346
  14.6 0.0 copy-start.5
  14.6 0.0 copy-start.6
  14.6 0.0 copy-done
  14.7 0.0 copy-done.2
  14.7 2.1 %copy.19.rel = f32[1280,400]{1,0:T(8,128)S(1)} copy(f32[1280,400]{0,1:T(8,128)} %param.15) | data formatting | bytes 4096000 | tf_op args[4]
  16.7 12.7 %bucket.1 = (bf16[256,400]{1,0:T(8,128)(2,1)S(1)}, bf16[128,400]{1,0:T(8,128)(2,1)S(1)}, bf16[1280,400]{1,0:T(8,128)(2,1)S(1)}) custom-call(bf16[256,400]{1,0:T(8,128)(2,1)S(1)} %get-tuple-element.14.srows, bf16[128,400]{1,0:T(8,128)(2,1)S(1)} %get-tuple-element.15.drows, f32[1280,400]{1,0:T(8,128)S(1)} %copy.19.rel, s32[3,2048]{1,0:T(4,128)S(1)} %copy-done.5, ...), custom_call_target="tpu_custom_call" | custom-call | tf_op jit(solution)/shard_map/bucket/pallas_call | solution.py:368
  29.4 0.0 copy-start.11
  29.5 0.0 copy-start.12
  29.5 40.1 %give_back.1 = (f32[512,400]{1,0:T(8,128)S(1)}, f32[512,400]{1,0:T(8,128)S(1)}, bf16[1280,400]{1,0:T(8,128)(2,1)S(1)}) custom-call(bf16[256,400]{1,0:T(8,128)(2,1)S(1)} %get-tuple-element.16.sgrad, bf16[128,400]{1,0:T(8,128)(2,1)S(1)} %get-tuple-element.17.tgrad, bf16[1280,400]{1,0:T(8,128)(2,1)S(1)} %get-tuple-element.18.rgrad, s32[4,64]{1,0:T(4,128)S(1)} %copy-done.7, ...), custom_call_target="tpu_custom_call" | custom-call | tf_op jit(solution)/shard_map/give_back/pallas_call | solution.py:395
  69.6 0.0 copy-start.4
  69.6 0.2 multiply_reduce_fusion.1
  69.8 0.2 multiply_reduce_fusion
  70.0 0.7 fusion.4
  70.7 0.6 fusion.5
  71.2 1.7 %divide_subtract_fusion = (f32[512,400]{1,0:T(8,128)}, f32[512,400]{1,0:T(8,128)}) fusion(f32[512,400]{1,0:T(8,128)S(1)} %copy-done.3, f32[512,400]{1,0:T(8,128)S(1)} %get-tuple-element.20, f32[512]{0:T(512)S(1)} %get-tuple-element.30, f32[512,400]{1,0:T(8,128)S(1)} %copy-done.1, f32[512]{0:T(512)S(1)} %get-tuple-element.32, f32[512,400]{1,0:T(8,128)S(1)} %get-tuple-element.19), kind=kLoop, calls=%fused_computation.5 | loop fusion | flops 1228800 | bytes 4919296 | tf_op jit(solution)/shard_map/sub | solution.py:319
  73.0 2.4 %copy.24 = f32[512,400]{0,1:T(8,128)} copy(f32[512,400]{1,0:T(8,128)} %get-tuple-element.34) | data formatting | bytes 1638400
  75.4 1.7 %fusion.2 = f32[1280]{0:T(1024)S(1)} fusion(bf16[1280,400]{1,0:T(8,128)(2,1)} %copy-done.4), kind=kLoop, calls=%fused_computation.4 | loop fusion | flops 1534720 | bytes 1029120 | tf_op jit(solution)/shard_map/reduce_sum | solution.py:318
  77.1 0.6 fusion.3
  77.7 3.2 %fusion.1 = f32[1280,400]{1,0:T(8,128)} fusion(f32[1280,400]{1,0:T(8,128)S(1)} %copy.19.rel, bf16[1280,400]{1,0:T(8,128)(2,1)} %copy-done.4, f32[1280]{0:T(1024)S(1)} %get-tuple-element.28), kind=kLoop, calls=%fused_computation.3 | loop fusion | flops 2048000 | bytes 5125120 | tf_op jit(solution)/shard_map/sub | solution.py:319
  80.9 3.1 %copy.25 = f32[1280,400]{0,1:T(8,128)} copy(f32[1280,400]{1,0:T(8,128)} %fusion.1) | data formatting | bytes 4096000
  84.1 1.2 %copy.23 = f32[512,400]{0,1:T(8,128)} copy(f32[512,400]{1,0:T(8,128)S(1)} %copy-done.9) | data formatting | bytes 1638400
  (19 shorter events, 0.0 us)
Async XLA Ops:
  0.6 4.0 %copy-start.8 = (s32[4,32]{1,0:T(4,128)S(1)}, s32[4,32]{1,0:T(4,128)}, u32[]{:S(2)}) copy-start(s32[4,32]{1,0:T(4,128)} %tlist.3) | copy-start | bytes 1540
  0.6 4.0 %copy-start.7 = (s32[4,64]{1,0:T(4,128)S(1)}, s32[4,64]{1,0:T(4,128)}, u32[]{:S(2)}) copy-start(s32[4,64]{1,0:T(4,128)} %slist.3) | copy-start | bytes 3076
  2.8 11.8 %copy-start = (f32[512,400]{1,0:T(8,128)}, f32[512,400]{1,0:T(8,128)S(1)}, u32[]{:S(2)}) copy-start(f32[512,400]{1,0:T(8,128)S(1)} %copy.20.stab) | copy-start | bytes 2457604
  4.7 10.0 %copy-start.2 = (f32[512,400]{1,0:T(8,128)}, f32[512,400]{1,0:T(8,128)S(1)}, u32[]{:S(2)}) copy-start(f32[512,400]{1,0:T(8,128)S(1)} %copy.18.ttab) | copy-start | bytes 2457604
  14.6 2.1 %copy-start.5 = (s32[3,2048]{1,0:T(4,128)S(1)}, s32[3,2048]{1,0:T(4,128)}, u32[]{:S(2)}) copy-start(s32[3,2048]{1,0:T(4,128)} %edges.1) | copy-start | bytes 73732
  14.6 2.1 %copy-start.6 = (s32[4,512]{1,0:T(4,128)S(1)}, s32[4,512]{1,0:T(4,128)}, u32[]{:S(2)}) copy-start(s32[4,512]{1,0:T(4,128)} %negs.1) | copy-start | bytes 24580
  29.4 40.5 %copy-start.11 = (f32[512]{0:T(512)S(1)}, f32[512]{0:T(512)}, u32[]{:S(2)}) copy-start(f32[512]{0:T(512)} %param.14) | copy-start | bytes 6148
  29.5 41.2 %copy-start.12 = (f32[512]{0:T(512)S(1)}, f32[512]{0:T(512)}, u32[]{:S(2)}) copy-start(f32[512]{0:T(512)} %param.12) | copy-start | bytes 6148
  29.5 41.8 %copy-start.1 = (f32[512,400]{1,0:T(8,128)S(1)}, f32[512,400]{1,0:T(8,128)}, u32[]{:S(2)}) copy-start(f32[512,400]{1,0:T(8,128)} %copy-done) | copy-start | bytes 2457604
  29.5 41.8 %copy-start.3 = (f32[512,400]{1,0:T(8,128)S(1)}, f32[512,400]{1,0:T(8,128)}, u32[]{:S(2)}) copy-start(f32[512,400]{1,0:T(8,128)} %copy-done.2) | copy-start | bytes 2457604
  69.6 3.3 %copy-start.4 = (bf16[1280,400]{1,0:T(8,128)(2,1)}, bf16[1280,400]{1,0:T(8,128)(2,1)S(1)}, u32[]{:S(2)}) copy-start(bf16[1280,400]{1,0:T(8,128)(2,1)S(1)} %get-tuple-element.21) | copy-start | bytes 3072004
  73.0 4.1 %copy-start.10 = (f32[1280]{0:T(1024)S(1)}, f32[1280]{0:T(1024)}, u32[]{:S(2)}) copy-start(f32[1280]{0:T(1024)} %param.16) | copy-start | bytes 15364
  80.9 3.1 %copy-start.9 = (f32[512,400]{1,0:T(8,128)S(1)}, f32[512,400]{1,0:T(8,128)}, u32[]{:S(2)}) copy-start(f32[512,400]{1,0:T(8,128)} %get-tuple-element.35) | copy-start | bytes 2457604

commit v2 on v1

v2 whole, which is shorter than its diff:
```python
import functools

import jax
import jax.numpy as jnp
from jax import lax
from jax.experimental import pallas as pl
from jax.experimental.pallas import tpu as pltpu
from jax.sharding import PartitionSpec as P

learn_rate = 0.1
MESH = pl.DeviceIdType.MESH
BF = jnp.bfloat16
F32 = jnp.float32


def dot(a, b):
    return jnp.dot(a, b, preferred_element_type=F32)


def dot_nt(a, b):
    return lax.dot_general(a, b, (((1,), (1,)), ((), ())), preferred_element_type=F32)


def dot_tn(a, b):
    return lax.dot_general(a, b, (((0,), (0,)), ((), ())), preferred_element_type=F32)


def one_hot(rows, ids):
    where = lax.broadcasted_iota(jnp.int32, (rows, ids.shape[1]), 0) == ids
    return jnp.where(where, 1.0, 0.0).astype(BF)


def greet(n_src, n_dst, me_s, me_d):
    barrier = pltpu.get_barrier_semaphore()
    for k in range(1, n_dst):
        pl.semaphore_signal(
            barrier, 1, device_id={"dst": lax.rem(me_d + k, n_dst)}, device_id_type=MESH
        )
    for k in range(1, n_src):
        pl.semaphore_signal(
            barrier, 1, device_id={"src": lax.rem(me_s + k, n_src)}, device_id_type=MESH
        )
    return barrier


def swap(axis, n, me, cap, out_ref, in_ref, send, recv):
    copies = []
    for k in range(1, n):
        peer = lax.rem(me + k, n)
        copy = pltpu.make_async_remote_copy(
            src_ref=out_ref.at[pl.ds(pl.multiple_of(peer * cap, cap), cap)],
            dst_ref=in_ref.at[pl.ds(pl.multiple_of(me * cap, cap), cap)],
            send_sem=send.at[k - 1],
            recv_sem=recv.at[k - 1],
            device_id={axis: peer},
            device_id_type=MESH,
        )
        copy.start()
        copies.append(copy)
    return copies


def row_of(lists):
    return jnp.concatenate([lists[p : p + 1, :] for p in range(lists.shape[0])], axis=1)


def step_kernel(
    n_src, n_dst, pieces, step,
    stab, ttab, rel, edges, count, negs, slist, tlist,
    ssum, tsum, total,
    sout, tout, sin, tin, sgrad, tgrad, sback, tback,
    relation_of, src_t, dst_t, hots, rg, packed,
    core_in, x_in, z_in, core_sum, x_sum, full,
    f1, f2, f3, f4, s1, r1, s2, r2,
    cs_s, cs_r, xs_s, xs_r, zs_s, zs_r, zg_s, zg_r, xg_s, xg_r, cg_s, cg_r,
):
    me_s = lax.axis_index("src")
    me_d = lax.axis_index("dst")
    core = lax.rem(me_d, 2)
    chip = me_d // 2
    chips = n_dst // 2
    other = me_d + 1 - 2 * core
    cs = slist.shape[1]
    cd = tlist.shape[1]
    own = stab.shape[1]
    slots = n_dst * cs
    targets = n_src * cd
    width, relations = rel.shape
    half = width // 2
    blocks, negatives = negs.shape
    span = edges.shape[1] // blocks
    z_rows = step
    x_rows = z_rows * n_src
    c_rows = x_rows * chips
    p_rows = c_rows * 2

    barrier = greet(n_src, n_dst, me_s, me_d)
    hot_target = one_hot(own, row_of(tlist))
    hot_source = one_hot(own, row_of(slist))
    tout[...] = dot(ttab[...].astype(BF), hot_target).astype(BF).T
    sout[...] = dot(stab[...].astype(BF), hot_source).astype(BF).T
    pl.semaphore_wait(barrier, n_src + n_dst - 2)
    second = swap("src", n_src, me_s, cd, tout, tin, f3, f4)
    first = swap("dst", n_dst, me_d, cs, sout, sin, f1, f2)
    mine_s = pl.ds(pl.multiple_of(me_d * cs, cs), cs)
    mine_d = pl.ds(pl.multiple_of(me_s * cd, cd), cd)
    sin[mine_s, :] = sout[mine_s, :]
    tin[mine_d, :] = tout[mine_d, :]

    table = rel[...]
    rel_high = table.astype(BF)
    rel_rest = (table - rel_high.astype(F32)).astype(BF)
    for c in range(blocks):
        cols = slice(c * span, (c + 1) * span)
        hot_r = one_hot(relations, edges[1:2, cols])
        hots[:, cols] = hot_r
        relation_of[:, cols] = dot(rel_high, hot_r) + dot(rel_rest, hot_r)

    for copy in second:
        copy.wait()
    for copy in first:
        copy.wait()
    src_t[...] = sin[...].T
    dst_t[...] = tin[...].T
    source_acc = jnp.zeros((slots, width), F32)
    target_acc = jnp.zeros((targets, width), F32)
    live = count[0]
    for c in range(blocks):
        cols = slice(c * span, (c + 1) * span)
        uses = one_hot(targets, negs[c : c + 1, :])
        uses = jnp.sum(uses.astype(F32), axis=1, keepdims=True)
        hot_s = one_hot(slots, edges[0:1, cols])
        is_target = (
            lax.broadcasted_iota(jnp.int32, (targets, span), 0) == edges[2:3, cols]
        )
        place = c * span + lax.broadcasted_iota(jnp.int32, (1, span), 1)
        alive = jnp.where(place < live, 1.0, 0.0)
        source = dot(src_t[...], hot_s)
        relation = relation_of[:, cols]
        sr, si = source[:half], source[half:]
        rr, ri = relation[:half], relation[half:]
        query = jnp.concatenate([sr * rr - si * ri, sr * ri + si * rr], axis=0)
        low = query.astype(BF)
        rest = (query - low.astype(F32)).astype(BF)
        logits = dot(tin[...], low)
        extra = dot(tin[...], rest)
        positive = jnp.sum(jnp.where(is_target, logits + extra, 0.0), axis=0, keepdims=True)
        pos_weight = -alive * jax.nn.sigmoid(-positive)
        neg_weight = (jax.nn.sigmoid(logits) * (alive / negatives)).astype(BF).astype(F32)
        weight = jnp.where(is_target, pos_weight, 0.0) + uses * neg_weight
        w_high = weight.astype(BF)
        w_rest = (weight - w_high.astype(F32)).astype(BF)
        grad = dot(dst_t[...], w_high) + dot(dst_t[...], w_rest)
        target_acc = target_acc + (
            dot_nt(w_high, low) + (dot_nt(w_rest, low) + dot_nt(w_high, rest))
        )
        gr, gi = grad[:half], grad[half:]
        source_grad = jnp.concatenate([gr * rr + gi * ri, gi * rr - gr * ri], axis=0)
        source_acc = source_acc + dot_nt(hot_s, source_grad.astype(BF))
        rg[:, cols] = jnp.concatenate(
            [gr * sr + gi * si, gi * sr - gr * si], axis=0
        ).astype(BF)

    def rows(start, count):
        return pl.ds(pl.multiple_of(start, 16), count)

    def push(src, dst, send, recv, axis, peer):
        copy = pltpu.make_async_remote_copy(
            src_ref=src, dst_ref=dst, send_sem=send, recv_sem=recv,
            device_id={axis: peer}, device_id_type=MESH,
        )
        copy.start()
        return copy

    started = {}

    def stage_core(p):
        started["c", p] = [
            push(
                packed.at[rows(p * p_rows + (1 - core) * c_rows, c_rows)],
                core_in.at[pl.ds(p * c_rows, c_rows)],
                cs_s.at[p], cs_r.at[p], "dst", other,
            )
        ]

    def stage_x(p):
        for copy in started["c", p]:
            copy.wait()
        here = pl.ds(p * c_rows, c_rows)
        own = packed[rows(p * p_rows + core * c_rows, c_rows), :]
        core_sum[here, :] = (own.astype(F32) + core_in[here, :].astype(F32)).astype(BF)
        started["x", p] = []
        for k in range(1, chips):
            peer = lax.rem(chip + k, chips)
            slot = p * (chips - 1) + k - 1
            started["x", p].append(
                push(
                    core_sum.at[rows(p * c_rows + peer * x_rows, x_rows)],
                    x_in.at[pl.ds(slot * x_rows, x_rows)],
                    xs_s.at[slot], xs_r.at[slot], "dst", peer * 2 + core,
                )
            )

    def stage_z(p):
        for copy in started["x", p]:
            copy.wait()
        value = core_sum[rows(p * c_rows + chip * x_rows, x_rows), :].astype(F32)
        for k in range(1, chips):
            slot = p * (chips - 1) + k - 1
            value = value + x_in[pl.ds(slot * x_rows, x_rows), :].astype(F32)
        x_sum[pl.ds(p * x_rows, x_rows), :] = value.astype(BF)
        started["z", p] = []
        for k in range(1, n_src):
            peer = lax.rem(me_s + k, n_src)
            slot = p * (n_src - 1) + k - 1
            started["z", p].append(
                push(
                    x_sum.at[rows(p * x_rows + peer * z_rows, z_rows)],
                    z_in.at[pl.ds(slot * z_rows, z_rows)],
                    zs_s.at[slot], zs_r.at[slot], "src", peer,
                )
            )

    def place(p, chip_at, src_at):
        return p * p_rows + core * c_rows + chip_at * x_rows + src_at * z_rows

    def gather_z(p):
        for copy in started["z", p]:
            copy.wait()
        value = x_sum[rows(p * x_rows + me_s * z_rows, z_rows), :].astype(F32)
        for k in range(1, n_src):
            slot = p * (n_src - 1) + k - 1
            value = value + z_in[pl.ds(slot * z_rows, z_rows), :].astype(F32)
        here = rows(place(p, chip, me_s), z_rows)
        full[here, :] = value.astype(BF)
        started["gz", p] = []
        for k in range(1, n_src):
            peer = lax.rem(me_s + k, n_src)
            slot = p * (n_src - 1) + k - 1
            started["gz", p].append(
                push(full.at[here], full.at[here], zg_s.at[slot], zg_r.at[slot], "src", peer)
            )

    def gather_x(p):
        for copy in started["gz", p]:
            copy.wait()
        here = rows(place(p, chip, 0), x_rows)
        started["gx", p] = []
        for k in range(1, chips):
            peer = lax.rem(chip + k, chips)
            slot = p * (chips - 1) + k - 1
            started["gx", p].append(
                push(
                    full.at[here], full.at[here], xg_s.at[slot], xg_r.at[slot],
                    "dst", peer * 2 + core,
                )
            )

    def gather_core(p):
        for copy in started["gx", p]:
            copy.wait()
        here = rows(place(p, 0, 0), c_rows)
        started["gc", p] = [
            push(full.at[here], full.at[here], cg_s.at[p], cg_r.at[p], "dst", other)
        ]

    def sums():
        for copy in back_s:
            copy.wait()
        ssum[...] = dot_nt(sback[...].T, hot_source)
        for copy in back_t:
            copy.wait()
        tsum[...] = dot_nt(tback[...].T, hot_target)

    used = (relations // 128) * width
    if packed.shape[0] > used:
        packed[used:, :] = jnp.zeros((packed.shape[0] - used, 128), BF)
    sent = 0
    for j in range(0, relations, 256):
        wide = min(256, relations - j)
        value = dot_nt(rg[...], hots[j : j + wide, :]).astype(BF)
        for i in range(0, wide, 128):
            at = ((j + i) // 128) * width
            packed[at : at + width, :] = value[:, i : i + 128]
        ready = ((j + wide) // 128) * width
        if j + wide == relations:
            ready = packed.shape[0]
        while sent < pieces and (sent + 1) * p_rows <= ready:
            stage_core(sent)
            if sent:
                stage_x(sent - 1)
            sent += 1
    stage_x(pieces - 1)
    sgrad[...] = source_acc.astype(BF)
    tgrad[...] = target_acc.astype(BF)
    back_s = swap("dst", n_dst, me_d, cs, sgrad, sback, s1, r1)
    back_t = swap("src", n_src, me_s, cd, tgrad, tback, s2, r2)
    sback[mine_s, :] = sgrad[mine_s, :]
    tback[mine_d, :] = tgrad[mine_d, :]
    for p in range(pieces):
        stage_z(p)
    for t in range(pieces + 2):
        if t < pieces:
            gather_z(t)
        if 0 <= t - 1 < pieces:
            gather_x(t - 1)
        if 0 <= t - 2 < pieces:
            gather_core(t - 2)
    sums()
    for p in range(pieces):
        for copy in started["gc", p]:
            copy.wait()
    total[...] = full[...]


def update_kernel(
    stab, sstate, ssum, ttab, tstate, tsum, rel, rstate, total,
    new_s, new_ss, new_t, new_ts, new_r, new_rs,
    out_s, out_t, out_r, sems,
):
    width, relations = rel.shape

    def update(table, state, grad):
        new_state = state + jnp.sum(grad * grad, axis=0, keepdims=True) / width
        return table - grad * (learn_rate / jnp.sqrt(new_state)), new_state

    copies = []

    def leave(src, dst):
        copy = pltpu.make_async_copy(src, dst, sems.at[len(copies)])
        copy.start()
        copies.append(copy)

    out_s[...], new_ss[...] = update(stab[...], sstate[...], ssum[...])
    leave(out_s, new_s)
    out_t[...], new_ts[...] = update(ttab[...], tstate[...], tsum[...])
    leave(out_t, new_t)
    for j in range(relations // 128):
        cols = slice(j * 128, (j + 1) * 128)
        out_r[:, cols], new_rs[:, cols] = update(
            rel[:, cols], rstate[:, cols], total[j * width : (j + 1) * width, :].astype(F32)
        )
        if j % 2 == 1 or j == relations // 128 - 1:
            done = slice((j - j % 2) * 128, (j + 1) * 128)
            leave(out_r.at[:, done], new_r.at[:, done])
    for copy in copies:
        copy.wait()


VM = pl.BlockSpec(memory_space=pltpu.VMEM)
SM = pl.BlockSpec(memory_space=pltpu.SMEM)
HB = pl.BlockSpec(memory_space=pl.ANY)
LIMIT = 48 * 1024 * 1024


def body(
    source_table, source_state, target_table, target_state, relation_table, relation_state,
    edge_list, edge_count, negative_ids, source_lists, target_lists,
):
    n_dst = lax.axis_size("dst")
    n_src = lax.axis_size("src")
    width = source_table.shape[1]
    cs = source_lists.shape[1]
    cd = target_lists.shape[1]
    own = source_table.shape[0]
    relations = relation_table.shape[0]
    edges = edge_list.shape[1]
    group = n_src * n_dst
    chips = n_dst // 2
    slots, targets = n_dst * cs, n_src * cd
    share = -(-(relations // 128) * width // (group * 16)) * 16
    step = 64 if share % 64 == 0 else share
    pieces = share // step
    padded = share * group
    x_rows = step * n_src
    c_rows = x_rows * chips
    x_n = pieces * (chips - 1)
    z_n = pieces * (n_src - 1)
    dma = pltpu.SemaphoreType.DMA
    flat_s, flat_t, flat_r = source_table.T, target_table.T, relation_table.T

    source_sum, target_sum, total = pl.pallas_call(
        functools.partial(step_kernel, n_src, n_dst, pieces, step),
        out_shape=[
            jax.ShapeDtypeStruct((width, own), F32),
            jax.ShapeDtypeStruct((width, own), F32),
            jax.ShapeDtypeStruct((padded, 128), BF),
        ],
        in_specs=[VM, VM, VM, VM, SM, VM, VM, VM],
        out_specs=[VM] * 3,
        scratch_shapes=[pltpu.VMEM((slots, width), BF), pltpu.VMEM((targets, width), BF)] * 4
        + [
            pltpu.VMEM((width, edges), F32),
            pltpu.VMEM((width, slots), BF),
            pltpu.VMEM((width, targets), BF),
            pltpu.VMEM((relations, edges), BF),
            pltpu.VMEM((width, edges), BF),
            pltpu.VMEM((padded, 128), BF),
            pltpu.VMEM((pieces * c_rows, 128), BF),
            pltpu.VMEM((x_n * x_rows, 128), BF),
            pltpu.VMEM((z_n * step, 128), BF),
            pltpu.VMEM((pieces * c_rows, 128), BF),
            pltpu.VMEM((pieces * x_rows, 128), BF),
            pltpu.VMEM((padded, 128), BF),
        ]
        + [dma((n_dst - 1,)), dma((n_dst - 1,)), dma((n_src - 1,)), dma((n_src - 1,))] * 2
        + [dma((n,)) for n in (pieces, pieces, x_n, x_n, z_n, z_n, z_n, z_n, x_n, x_n, pieces, pieces)],
        compiler_params=pltpu.CompilerParams(
            collective_id=0, has_side_effects=True, vmem_limit_bytes=LIMIT
        ),
        name="step",
    )(
        flat_s, flat_t, flat_r, edge_list, edge_count, negative_ids, source_lists, target_lists,
    )

    line = lambda n: jax.ShapeDtypeStruct((1, n), F32)
    new_s, new_ss, new_t, new_ts, new_r, new_rs = pl.pallas_call(
        update_kernel,
        out_shape=[
            jax.ShapeDtypeStruct((width, own), F32), line(own),
            jax.ShapeDtypeStruct((width, own), F32), line(own),
            jax.ShapeDtypeStruct((width, relations), F32), line(relations),
        ],
        in_specs=[VM] * 9,
        out_specs=[HB, VM] * 3,
        scratch_shapes=[
            pltpu.VMEM((width, own), F32),
            pltpu.VMEM((width, own), F32),
            pltpu.VMEM((width, relations), F32),
            dma((2 + (relations // 128 + 1) // 2,)),
        ],
        compiler_params=pltpu.CompilerParams(vmem_limit_bytes=LIMIT),
        name="update",
    )(
        flat_s, source_state[None], source_sum, flat_t, target_state[None], target_sum,
        flat_r, relation_state[None], total,
    )
    return (new_s.T, new_ss[0], new_t.T, new_ts[0], new_r.T, new_rs[0])


def solution(mesh):
    every = ("groups", "src", "dst")
    rows = P(every, None)
    flat = P(every)
    outs = (rows, flat, rows, flat, P("groups", None), P("groups"))
    return jax.shard_map(
        body,
        mesh=mesh,
        in_specs=outs + (P(None, every), flat, rows, rows, rows),
        out_specs=outs,
        check_vma=False,
    )
```

time: 85.6 us -> 60.5 us (0.71)
  Pallas kernels: 62.7 us -> 52.2 us
  other arithmetic: 8.81 us -> 0.62 us
  local copies, waits for them, and re-layouts: 12.2 us -> 5.81 us
    pallas_call x3 -> x2, Pallas kernels: 62.7 us -> 52.2 us  [the longest x1 48 us: body(): pl.pallas_call(functools.partial(step_kernel, n_src, n_dst, pieces, step)...]
    unnamed x32 -> x16, local copies, waits for them, and re-layouts: 12.2 us -> 5.11 us
    sub x2 -> x0, other arithmetic: 4.98 us -> none  [update_rows(): return (table - learn_rate * grad / jnp.sqrt(new_state)[:, None], new_state)]
    reduce_sum x3 -> x0, other arithmetic: 1.97 us -> none  [update_rows(): new_state = state + jnp.mean(grad * grad, axis=1)]
    sqrt x3 -> x0, other arithmetic: 1.87 us -> none  [update_rows(): return (table - learn_rate * grad / jnp.sqrt(new_state)[:, None], new_state)]
where the time goes in v2:
time: 60.5 us; the launch traced here: 60 us
  Pallas kernels  52.2 us (86%)
  local copies, waits for them, and re-layouts  5.81 us (10%)
  between operations  1.35 us (2%)
  other arithmetic  0.62 us (1%)
    pallas_call x1, Pallas kernels, body(): pl.pallas_call(functools.partial(step_kernel, n_src, n_dst, pieces, step)...  48 us
    unnamed x16, local copies, waits for them, and re-layouts  5.11 us
    pallas_call x1, Pallas kernels, body(): pl.pallas_call(update_kernel, out_shape=[jax.ShapeDtypeStruct((width, own...  4.24 us

profile of v2, /device:TPU:0, one launch (start us, length us, event | category | flops | bytes accessed | tf_op | source)
XLA Modules:
  0.0 60.0 jit_solution(8254759512417900998)
XLA Ops:
  0.6 0.0 copy-start.7
  0.6 0.0 copy-start.6
  1.3 0.7 %broadcast_in_dim.11.rstate = f32[1,1280]{1,0:T(1,128)S(1)} reshape(f32[1280]{0:T(1024)} %param.16) | data formatting | bytes 10240 | tf_op jit(solution)/shard_map/broadcast_in_dim | solution.py:436
  2.0 0.0 copy-start
  2.0 1.1 %copy-done = f32[512,400]{0,1:T(8,128)S(1)} copy-done((f32[512,400]{0,1:T(8,128)S(1)}, f32[512,400]{0,1:T(8,128)}, u32[]{:S(2)}) %copy-start) | copy-done | bytes 819224
  3.2 0.0 copy-start.1
  3.2 1.1 %copy-done.1 = f32[512,400]{0,1:T(8,128)S(1)} copy-done((f32[512,400]{0,1:T(8,128)S(1)}, f32[512,400]{0,1:T(8,128)}, u32[]{:S(2)}) %copy-start.1) | copy-done | bytes 819224
  4.3 0.0 copy-start.2
  4.3 0.8 %copy-done.2 = s32[3,2048]{1,0:T(4,128)S(1)} copy-done((s32[3,2048]{1,0:T(4,128)S(1)}, s32[3,2048]{1,0:T(4,128)}, u32[]{:S(2)}) %copy-start.2) | copy-done | bytes 24600
  5.1 0.0 copy-start.3
  5.1 0.7 %copy-done.3 = s32[4,512]{1,0:T(4,128)S(1)} copy-done((s32[4,512]{1,0:T(4,128)S(1)}, s32[4,512]{1,0:T(4,128)}, u32[]{:S(2)}) %copy-start.3) | copy-done | bytes 8216
  5.8 0.0 copy-start.4
  5.8 0.7 %copy-done.4 = s32[4,64]{1,0:T(4,128)S(1)} copy-done((s32[4,64]{1,0:T(4,128)S(1)}, s32[4,64]{1,0:T(4,128)}, u32[]{:S(2)}) %copy-start.4) | copy-done | bytes 1048
  6.4 0.0 copy-start.5
  6.5 0.7 %copy-done.5 = s32[4,32]{1,0:T(4,128)S(1)} copy-done((s32[4,32]{1,0:T(4,128)S(1)}, s32[4,32]{1,0:T(4,128)}, u32[]{:S(2)}) %copy-start.5) | copy-done | bytes 536
  7.1 48.0 %step.1 = (f32[400,512]{1,0:T(8,128)S(1)}, f32[400,512]{1,0:T(8,128)S(1)}, bf16[4096,128]{1,0:T(8,128)(2,1)S(1)}) custom-call(f32[400,512]{1,0:T(8,128)S(1)} %bitcast.10, f32[400,512]{1,0:T(8,128)S(1)} %bitcast.12, f32[400,1280]{1,0:T(8,128)} %bitcast.16, s32[3,2048]{1,0:T(4,128)S(1)} %copy-done.2, s32[1]{0:T(128)S(6)} %copy.17.count, ...), custom_call_target="tpu_custom_call" | custom-call | tf_op jit(solution)/shard_map/step/pallas_call | solution.py:382
  55.1 0.0 copy-done.7
  55.1 0.0 copy-done.6
  55.1 4.2 %update.1 = (f32[400,512]{1,0:T(8,128)}, f32[1,512]{1,0:T(1,128)}, f32[400,512]{1,0:T(8,128)}, f32[1,512]{1,0:T(1,128)}, f32[400,1280]{1,0:T(8,128)}, /*index=5*/f32[1,1280]{1,0:T(1,128)S(1)}) custom-call(f32[400,512]{1,0:T(8,128)S(1)} %bitcast.11, f32[1,512]{1,0:T(1,128)S(1)} %bitcast.14, f32[400,512]{1,0:T(8,128)S(1)} %get-tuple-element.15.ssum, ...), custom_call_target="tpu_custom_call" | custom-call | tf_op jit(solution)/shard_map/update/pallas_call | solution.py:417
  59.4 0.6 %reduce = f32[1280]{0:T(1024)} reduce(f32[1,1280]{1,0:T(1,128)S(1)} %get-tuple-element.23, f32[]{:T(128)} %constant.4), dimensions={0}, to_apply=%get-tuple-element.23.reduce_sub_computation | reduce | bytes 10244 | tf_op jit(solution)/shard_map/update/pallas_call | solution.py:417
Async XLA Ops:
  0.6 54.5 %copy-start.7 = (f32[512]{0:T(512)S(1)}, f32[512]{0:T(512)}, u32[]{:S(2)}) copy-start(f32[512]{0:T(512)} %param.14) | copy-start | bytes 6148
  0.6 54.5 %copy-start.6 = (f32[512]{0:T(512)S(1)}, f32[512]{0:T(512)}, u32[]{:S(2)}) copy-start(f32[512]{0:T(512)} %param.12) | copy-start | bytes 6148
  2.0 1.1 %copy-start = (f32[512,400]{0,1:T(8,128)S(1)}, f32[512,400]{0,1:T(8,128)}, u32[]{:S(2)}) copy-start(f32[512,400]{0,1:T(8,128)} %param.11) | copy-start | bytes 2457604
  3.2 1.1 %copy-start.1 = (f32[512,400]{0,1:T(8,128)S(1)}, f32[512,400]{0,1:T(8,128)}, u32[]{:S(2)}) copy-start(f32[512,400]{0,1:T(8,128)} %param.13) | copy-start | bytes 2457604
  4.3 0.8 %copy-start.2 = (s32[3,2048]{1,0:T(4,128)S(1)}, s32[3,2048]{1,0:T(4,128)}, u32[]{:S(2)}) copy-start(s32[3,2048]{1,0:T(4,128)} %edges.1) | copy-start | bytes 73732
  5.1 0.7 %copy-start.3 = (s32[4,512]{1,0:T(4,128)S(1)}, s32[4,512]{1,0:T(4,128)}, u32[]{:S(2)}) copy-start(s32[4,512]{1,0:T(4,128)} %negs.1) | copy-start | bytes 24580
  5.8 0.7 %copy-start.4 = (s32[4,64]{1,0:T(4,128)S(1)}, s32[4,64]{1,0:T(4,128)}, u32[]{:S(2)}) copy-start(s32[4,64]{1,0:T(4,128)} %slist.1) | copy-start | bytes 3076
  6.4 0.7 %copy-start.5 = (s32[4,32]{1,0:T(4,128)S(1)}, s32[4,32]{1,0:T(4,128)}, u32[]{:S(2)}) copy-start(s32[4,32]{1,0:T(4,128)} %tlist.1) | copy-start | bytes 1540

commit v3 on v2

--- a/solution.py
+++ b/solution.py
@@ -66,8 +66,9 @@
 
 def step_kernel(
     n_src, n_dst, pieces, step,
-    stab, ttab, rel, edges, count, negs, slist, tlist,
-    ssum, tsum, total,
+    stab_at, ttab_at, rel_at, edges_at, count, negs_at, slist_at, tlist_at,
+    ssum_at, tsum_at, total_at,
+    ssum, tsum, out_sems, stab, ttab, rel, edges, negs, slist, tlist, in_sems,
     sout, tout, sin, tin, sgrad, tgrad, sback, tback,
     relation_of, src_t, dst_t, hots, rg, packed,
     core_in, x_in, z_in, core_sum, x_sum, full,
@@ -94,10 +95,22 @@
     c_rows = x_rows * chips
     p_rows = c_rows * 2
 
+    loads = []
+    for src, dst in (
+        (tlist_at, tlist), (ttab_at, ttab), (slist_at, slist), (stab_at, stab),
+        (edges_at, edges), (rel_at, rel), (negs_at, negs),
+    ):
+        load = pltpu.make_async_copy(src, dst, in_sems.at[len(loads)])
+        load.start()
+        loads.append(load)
     barrier = greet(n_src, n_dst, me_s, me_d)
+    loads[0].wait()
+    loads[1].wait()
     hot_target = one_hot(own, row_of(tlist))
+    tout[...] = dot(ttab[...].astype(BF), hot_target).astype(BF).T
+    loads[2].wait()
+    loads[3].wait()
     hot_source = one_hot(own, row_of(slist))
-    tout[...] = dot(ttab[...].astype(BF), hot_target).astype(BF).T
     sout[...] = dot(stab[...].astype(BF), hot_source).astype(BF).T
     pl.semaphore_wait(barrier, n_src + n_dst - 2)
     second = swap("src", n_src, me_s, cd, tout, tin, f3, f4)
@@ -107,6 +120,8 @@
     sin[mine_s, :] = sout[mine_s, :]
     tin[mine_d, :] = tout[mine_d, :]
 
+    for load in loads[4:]:
+        load.wait()
     table = rel[...]
     rel_high = table.astype(BF)
     rel_rest = (table - rel_high.astype(F32)).astype(BF)
@@ -173,6 +188,13 @@
         return copy
 
     started = {}
+    leaving = []
+
+    def leave(src, dst):
+        copy = pltpu.make_async_copy(src, dst, out_sems.at[len(leaving)])
+        copy.start()
+        leaving.append(copy)
+
 
     def stage_core(p):
         started["c", p] = [
@@ -268,9 +290,11 @@
         for copy in back_s:
             copy.wait()
         ssum[...] = dot_nt(sback[...].T, hot_source)
+        leave(ssum, ssum_at)
         for copy in back_t:
             copy.wait()
         tsum[...] = dot_nt(tback[...].T, hot_target)
+        leave(tsum, tsum_at)
 
     used = (relations // 128) * width
     if packed.shape[0] > used:
@@ -299,6 +323,7 @@
     tback[mine_d, :] = tgrad[mine_d, :]
     for p in range(pieces):
         stage_z(p)
+    sums()
     for t in range(pieces + 2):
         if t < pieces:
             gather_z(t)
@@ -306,11 +331,13 @@
             gather_x(t - 1)
         if 0 <= t - 2 < pieces:
             gather_core(t - 2)
-    sums()
     for p in range(pieces):
         for copy in started["gc", p]:
             copy.wait()
-    total[...] = full[...]
+        done = pl.ds(p * p_rows, p_rows)
+        leave(full.at[done], total_at.at[done])
+    for copy in leaving:
+        copy.wait()
 
 
 def update_kernel(
@@ -331,15 +358,18 @@
         copy.start()
         copies.append(copy)
 
-    out_s[...], new_ss[...] = update(stab[...], sstate[...], ssum[...])
+    out_s[...], state = update(stab[...], sstate[...][None], ssum[...])
+    new_ss[...] = state[0]
     leave(out_s, new_s)
-    out_t[...], new_ts[...] = update(ttab[...], tstate[...], tsum[...])
+    out_t[...], state = update(ttab[...], tstate[...][None], tsum[...])
+    new_ts[...] = state[0]
     leave(out_t, new_t)
     for j in range(relations // 128):
         cols = slice(j * 128, (j + 1) * 128)
-        out_r[:, cols], new_rs[:, cols] = update(
-            rel[:, cols], rstate[:, cols], total[j * width : (j + 1) * width, :].astype(F32)
-        )
+        out_r[:, cols], state = update(
+            rel[:, cols], rstate[cols][None], total[j * width : (j + 1) * width, :].astype(F32)
+        )
+        new_rs[cols] = state[0]
         if j % 2 == 1 or j == relations // 128 - 1:
             done = slice((j - j % 2) * 128, (j + 1) * 128)
             leave(out_r.at[:, done], new_r.at[:, done])
@@ -350,7 +380,7 @@
 VM = pl.BlockSpec(memory_space=pltpu.VMEM)
 SM = pl.BlockSpec(memory_space=pltpu.SMEM)
 HB = pl.BlockSpec(memory_space=pl.ANY)
-LIMIT = 48 * 1024 * 1024
+LIMIT = 58 * 1024 * 1024
 
 
 def body(
@@ -369,7 +399,7 @@
     chips = n_dst // 2
     slots, targets = n_dst * cs, n_src * cd
     share = -(-(relations // 128) * width // (group * 16)) * 16
-    step = 64 if share % 64 == 0 else share
+    step = 128 if share % 128 == 0 else share
     pieces = share // step
     padded = share * group
     x_rows = step * n_src
@@ -386,9 +416,21 @@
             jax.ShapeDtypeStruct((width, own), F32),
             jax.ShapeDtypeStruct((padded, 128), BF),
         ],
-        in_specs=[VM, VM, VM, VM, SM, VM, VM, VM],
-        out_specs=[VM] * 3,
-        scratch_shapes=[pltpu.VMEM((slots, width), BF), pltpu.VMEM((targets, width), BF)] * 4
+        in_specs=[HB, HB, HB, HB, SM, HB, HB, HB],
+        out_specs=[HB] * 3,
+        scratch_shapes=[
+            pltpu.VMEM((width, own), F32),
+            pltpu.VMEM((width, own), F32),
+            dma((2 + pieces,)),
+        ]
+        + [
+            pltpu.VMEM(x.shape, x.dtype)
+            for x in (
+                flat_s, flat_t, flat_r, edge_list, negative_ids, source_lists, target_lists
+            )
+        ]
+        + [dma((7,))]
+        + [pltpu.VMEM((slots, width), BF), pltpu.VMEM((targets, width), BF)] * 4
         + [
             pltpu.VMEM((width, edges), F32),
             pltpu.VMEM((width, slots), BF),
@@ -413,7 +455,7 @@
         flat_s, flat_t, flat_r, edge_list, edge_count, negative_ids, source_lists, target_lists,
     )
 
-    line = lambda n: jax.ShapeDtypeStruct((1, n), F32)
+    line = lambda n: jax.ShapeDtypeStruct((n,), F32)
     new_s, new_ss, new_t, new_ts, new_r, new_rs = pl.pallas_call(
         update_kernel,
         out_shape=[
@@ -432,10 +474,10 @@
         compiler_params=pltpu.CompilerParams(vmem_limit_bytes=LIMIT),
         name="update",
     )(
-        flat_s, source_state[None], source_sum, flat_t, target_state[None], target_sum,
-        flat_r, relation_state[None], total,
+        flat_s, source_state, source_sum, flat_t, target_state, target_sum,
+        flat_r, relation_state, total,
     )
-    return (new_s.T, new_ss[0], new_t.T, new_ts[0], new_r.T, new_rs[0])
+    return (new_s.T, new_ss, new_t.T, new_ts, new_r.T, new_rs)
 
 
 def solution(mesh):

time: 60.5 us -> 51.3 us (0.85)
  local copies, waits for them, and re-layouts: 5.81 us -> 0 us
  Pallas kernels: 52.2 us -> 49.9 us
  other arithmetic: 0.62 us -> 0 us
    unnamed x16 -> x0, local copies, waits for them, and re-layouts: 5.11 us -> none
    pallas_call x1, Pallas kernels: 48 us -> 44.3 us  [body(): pl.pallas_call(functools.partial(step_kernel, n_src, n_dst, pieces, step)...]
    pallas_call x1, Pallas kernels: 4.24 us -> 5.56 us  [body(): pl.pallas_call(update_kernel, out_shape=[jax.ShapeDtypeStruct((width, own...]
    broadcast_in_dim x1 -> x0, local copies, waits for them, and re-layouts: 0.7 us -> none  [body(): relation_state[None]]
    pallas_call x1 -> x0, other arithmetic: 0.62 us -> none  [body(): pl.pallas_call(update_kernel, out_shape=[jax.ShapeDtypeStruct((width, own...]
where the time goes in v3:
time: 51.3 us; the launch traced here: 51.1 us
  Pallas kernels  49.9 us (97%)
  between operations  1.29 us (3%)
    pallas_call x1, Pallas kernels, body(): pl.pallas_call(functools.partial(step_kernel, n_src, n_dst, pieces, step)...  44.3 us
    pallas_call x1, Pallas kernels, body(): pl.pallas_call(update_kernel, out_shape=[jax.ShapeDtypeStruct((width, own...  5.56 us

profile of v3, /device:TPU:0, one launch (start us, length us, event | category | flops | bytes accessed | tf_op | source)
XLA Modules:
  0.0 51.1 jit_solution(16151725921234733646)
XLA Ops:
  1.3 44.3 %step.1 = (f32[400,512]{1,0:T(8,128)}, f32[400,512]{1,0:T(8,128)}, bf16[4096,128]{1,0:T(8,128)(2,1)}) custom-call(f32[400,512]{1,0:T(8,128)} %bitcast.8, f32[400,512]{1,0:T(8,128)} %bitcast.10, f32[400,1280]{1,0:T(8,128)} %bitcast.6, s32[3,2048]{1,0:T(4,128)} %edges_at.1, s32[1]{0:T(128)S(6)} %copy.17.count, s32[4,512]{1,0:T(4,128)} %negs_at.1, ...), custom_call_target="tpu_custom_call" | custom-call | tf_op jit(solution)/shard_map/step/pallas_call | solution.py:412
  45.6 5.6 %update.1 = (f32[400,512]{1,0:T(8,128)}, f32[512]{0:T(512)}, f32[400,512]{1,0:T(8,128)}, f32[512]{0:T(512)}, f32[400,1280]{1,0:T(8,128)}, /*index=5*/f32[1280]{0:T(1024)}) custom-call(f32[400,512]{1,0:T(8,128)} %bitcast.9, f32[512]{0:T(512)} %sstate.1, f32[400,512]{1,0:T(8,128)} %get-tuple-element.15.ssum, f32[400,512]{1,0:T(8,128)} %bitcast.11, f32[512]{0:T(512)} %tstate.1, ...), custom_call_target="tpu_custom_call" | custom-call | tf_op jit(solution)/shard_map/update/pallas_call | solution.py:459
